TPU v7x, 32 devices: a whole 2x2x4 slice. The times are simulated.
32 devices in a mesh: tm: 8 (over z, y), dom: 4 (over x, core).
Axes of the slice: x: 2, y: 2, z: 4, core: 2. Of those that a mesh axis runs over, the one named last changes fastest.
Arguments:
- starting_voltage_guess: float32 [128, 4, 128], P('tm', 'dom'), may hold values from -3 to 3
- injected_amperes: float32 [128, 4, 128], P('tm', 'dom'), may hold values from -6 to 6
- capacitance: float32 [4, 128], P('dom'), may hold values from 0.5 to 2
- conductance: float32 [4, 128, 128], P('dom'), may hold values from -0.5 to 0.5
- block_pattern: int32 [4, 1, 1], P('dom'), may hold values 0 or 1
- device_gain: float32 [4, 128], P('dom'), may hold values from 0.2 to 2
- link_weight: float32 [4, 128, 128], P('dom'), may hold values from -0.5 to 0.5
- boundary_vertex_list: int32 [4, 128], P('dom'), may hold values from 0 to 127, as said below
- diagonal_reciprocals: float32 [128, 4, 1, 128, 128], P('tm', 'dom')
- boundary_jacobian: float32 [4, 128, 128], P('dom'), may hold values from -6 to 6
- transfer: float32 [128, 4, 1, 128, 128], P('tm', 'dom')
Outputs:
- periodic_state: float32 [128, 4, 128], P('tm', 'dom')
Inputs may be any that keep to these rules, and one draw needn't show every extreme that they name: `boundary_vertex_list`: the 128 interface nodes of one partition are distinct.
All inputs are finite; a program needn't handle non-finite values. No bound on the sum of `block_pattern` on one device may be relied on, other than what follows from the above.
Results may differ from a plain program's by a relative error of at most 0.0003.
Values sent between devices are 32-bit elements; how exact they have to be, the bound alone decides.
No kernel may reach another device: no remote copies, remote signals or barrier semaphores. Data moves between devices by JAX's collectives and lax.ppermute only.
A program may use at most 64 MiB of HBM per device.

v0:
```python
import functools

import jax
import jax.numpy as jnp
from jax import lax
from jax.experimental import pallas as pl
from jax.experimental.pallas import tpu as pltpu
from jax.sharding import PartitionSpec as P

ITERS = 2
F32 = jnp.float32
BF16 = jnp.bfloat16


def halves(x):
    hi = x.astype(BF16)
    return hi, (x - hi.astype(F32)).astype(BF16)


def split_cols(matrix):
    return jnp.concatenate(halves(matrix), axis=1)


def split_rows(vectors):
    hi, lo = halves(vectors)
    hi, lo = hi.astype(F32), lo.astype(F32)
    top = jnp.concatenate([hi, hi], axis=1)
    low = jnp.concatenate([lo, jnp.zeros_like(lo)], axis=1)
    return jnp.concatenate([top, low], axis=0).astype(BF16)


def dot_nt(a, b):
    return lax.dot_general(a, b, (((1,), (1,)), ((), ())), preferred_element_type=F32)


def times(a, b):
    ah, al = halves(a)
    bh, bl = halves(b)
    left = jnp.concatenate([ah, al, ah], axis=1)
    right = jnp.concatenate([bh, bh, bl], axis=0)
    return jnp.dot(left, right, preferred_element_type=F32)


def mapped(matrix_split, vectors):
    count = vectors.shape[0]
    both = dot_nt(split_rows(vectors), matrix_split)
    return both[:count] + both[count:]


def mapped_each(matrices_split, vectors):
    count, width = vectors.shape
    both = dot_nt(matrices_split, split_rows(vectors)).reshape(count, width, 2 * count)
    lane = lax.broadcasted_iota(jnp.int32, (width, 2 * count), 1) % count
    picked = jnp.zeros((width, 2 * count), F32)
    for r in range(count):
        picked = jnp.where(lane == r, both[r], picked)
    rows = picked.T
    return rows[:count] + rows[count:]


def call(kernel, outs, *args):
    vmem = pl.BlockSpec(memory_space=pltpu.VMEM)
    return pl.pallas_call(
        kernel,
        out_shape=[jax.ShapeDtypeStruct(s, d) for s, d in outs],
        in_specs=[vmem] * len(args),
        out_specs=[vmem] * len(outs),
        compiler_params=pltpu.CompilerParams(vmem_limit_bytes=24 * 2**20),
    )(*args)


def suffix_kernel(r_ref, s_ref, w_ref):
    points, width = r_ref.shape[0], r_ref.shape[1]
    u = [r_ref[i] for i in range(points)]
    span = 1
    while span < points:
        for base in range(0, points, 2 * span):
            mid = u[base + span]
            prod = times(mid, jnp.concatenate(u[base : base + span], axis=1))
            for i in range(span):
                u[base + i] = prod[:, i * width : (i + 1) * width]
        span *= 2
    w_ref[...] = u[0]
    for i in range(points - 1):
        s_ref[i * width : (i + 1) * width, :] = split_cols(u[i + 1])
    eye = (
        lax.broadcasted_iota(jnp.int32, (width, width), 0)
        == lax.broadcasted_iota(jnp.int32, (width, width), 1)
    ).astype(F32)
    s_ref[(points - 1) * width :, :] = split_cols(eye)


def prefix_kernel(r_ref, p_ref, l_ref):
    points, width = r_ref.shape[0], r_ref.shape[1]
    q = [r_ref[i] for i in range(points)]
    span, level, half = 1, 0, points // 2
    while span < points:
        slot = 0
        for base in range(0, points, 2 * span):
            upper = q[base + span : base + 2 * span]
            for matrix in upper:
                row = (level * half + slot) * width
                l_ref[row : row + width, :] = split_cols(matrix)
                slot += 1
            prod = times(jnp.concatenate(upper, axis=0), q[base + span - 1])
            for i in range(span):
                q[base + span + i] = prod[i * width : (i + 1) * width]
        span *= 2
        level += 1
    for i in range(points):
        p_ref[i * width : (i + 1) * width, :] = split_cols(q[i])


def scan_kernel(c_ref, l_ref, x_ref):
    points, width = c_ref.shape
    half = points // 2
    x = [c_ref[i : i + 1, :] for i in range(points)]
    span, level = 1, 0
    while span < points:
        heads = []
        for base in range(0, points, 2 * span):
            heads.extend([x[base + span - 1]] * span)
        moved = mapped_each(
            l_ref[level * half * width : (level + 1) * half * width, :],
            jnp.concatenate(heads, axis=0),
        )
        slot = 0
        for base in range(0, points, 2 * span):
            for i in range(base + span, base + 2 * span):
                x[i] = x[i] + moved[slot : slot + 1, :]
                slot += 1
        span *= 2
        level += 1
    x_ref[...] = jnp.concatenate(x, axis=0)


def prepare_kernel(d_ref, j_ref, k_ref, g_ref, mask_ref, ds_ref, js_ref, ks_ref, gs_ref):
    points, width = d_ref.shape[0], d_ref.shape[1]
    for i in range(points):
        ds_ref[i * width : (i + 1) * width, :] = split_cols(d_ref[i])
    js_ref[...] = split_cols(j_ref[...])
    ks_ref[...] = split_cols(k_ref[...])
    gs_ref[...] = split_cols(g_ref[...] * mask_ref[...].astype(F32))


def taken(rows, lanes):
    return jnp.take_along_axis(rows, jnp.broadcast_to(lanes, rows.shape), axis=1)


def first_half_of_step(s, halo, inj, cap, gain, gs_ref, ds_ref, bnd_ref, nr_ref, c_ref, msg_ref):
    points = s.shape[0]
    before = jnp.concatenate([halo, s[: points - 1]], axis=0)
    nr = inj - cap * (s - before) - mapped(gs_ref[...], s) - gain * jnp.tanh(s)
    c = mapped_each(ds_ref[...], nr)
    nr_ref[...] = nr
    c_ref[...] = c
    msg_ref[:points] = taken(c, bnd_ref[...])
    msg_ref[points:] = taken(s, bnd_ref[...])


def start_kernel(
    halo_ref, s_ref, inj_ref, cap_ref, gain_ref, gs_ref, ds_ref, bnd_ref, nr_ref, c_ref, msg_ref
):
    first_half_of_step(
        s_ref[...], halo_ref[...], inj_ref[...], cap_ref[...], gain_ref[...],
        gs_ref, ds_ref, bnd_ref, nr_ref, c_ref, msg_ref,
    )


def inflow_applied(got_ref, nr_ref, ds_ref, js_ref, ks_ref):
    points = nr_ref.shape[0]
    got = got_ref[...]
    nr = nr_ref[...] + mapped(js_ref[...], got[:points]) + mapped(ks_ref[...], got[points:])
    return mapped_each(ds_ref[...], nr)


def hop_kernel(
    place, got_ref, c_ref, msg_ref, nr_ref, ds_ref, js_ref, ks_ref, bnd_ref, new_c_ref, new_msg_ref
):
    points = c_ref.shape[0]
    here = lax.axis_index("dom") == place
    new_msg_ref[points:] = msg_ref[points:]

    @pl.when(here)
    def _():
        c = inflow_applied(got_ref, nr_ref, ds_ref, js_ref, ks_ref)
        new_c_ref[...] = c
        new_msg_ref[:points] = taken(c, bnd_ref[...])

    @pl.when(jnp.logical_not(here))
    def _():
        new_c_ref[...] = c_ref[...]
        new_msg_ref[:points] = msg_ref[:points]


def last_hop_kernel(
    place, got_ref, c_ref, nr_ref, ds_ref, js_ref, ks_ref, ss_ref, new_c_ref, tail_ref, f_ref
):
    points, width = c_ref.shape
    here = lax.axis_index("dom") == place

    @pl.when(here)
    def _():
        new_c_ref[...] = inflow_applied(got_ref, nr_ref, ds_ref, js_ref, ks_ref)

    @pl.when(jnp.logical_not(here))
    def _():
        new_c_ref[...] = c_ref[...]

    total = mapped_each(ss_ref[...], new_c_ref[...])
    shift = 1
    while shift < points:
        total = total + jnp.concatenate([total[shift:], jnp.zeros((shift, width), F32)], axis=0)
        shift *= 2
    tail_ref[:points] = jnp.concatenate([total[1:], jnp.zeros((1, width), F32)], axis=0)
    tail_ref[points:] = jnp.broadcast_to(total[:1], (8, width))
    f_ref[...] = jnp.broadcast_to(total[:1], (8, width))


def is_later(distance):
    return (lax.axis_index("tm") // distance) % 2 == 1


def first_level_kernel(
    distance, mw_ref, mf_ref, gw_ref, gf_ref,
    tw_ref, tf_ref, a_ref, bw_ref, bf_ref, aw_ref, af_ref,
):
    width = mw_ref.shape[0]
    later = is_later(distance)
    mw, mf, gw, gf = mw_ref[...], mf_ref[...], gw_ref[...], gf_ref[...]
    a = jnp.where(later, mw, gw)
    tw_ref[...] = times(a, jnp.where(later, gw, mw))
    a_split = split_cols(a)
    a_ref[...] = a_split
    tf_ref[...] = mapped(a_split, jnp.where(later, gf, mf)) + jnp.where(later, mf, gf)
    eye = (
        lax.broadcasted_iota(jnp.int32, (width, width), 0)
        == lax.broadcasted_iota(jnp.int32, (width, width), 1)
    ).astype(F32)
    bw_ref[...] = jnp.where(later, gw, eye)
    bf_ref[...] = jnp.where(later, gf, 0.0)
    aw_ref[...] = jnp.where(later, eye, gw)
    af_ref[...] = jnp.where(later, 0.0, gf)


def next_level_kernel(
    distance, mw_ref, mf_ref, gw_ref, gf_ref, bw_ref, bf_ref, aw_ref, af_ref,
    tw_ref, tf_ref, a_ref, x_ref, nbw_ref, nbf_ref, naw_ref, naf_ref,
):
    later = is_later(distance)
    mw, mf, gw, gf = mw_ref[...], mf_ref[...], gw_ref[...], gf_ref[...]
    bw, bf, aw, af = bw_ref[...], bf_ref[...], aw_ref[...], af_ref[...]
    a = jnp.where(later, mw, gw)
    tw_ref[...] = times(a, jnp.where(later, gw, mw))
    a_split = split_cols(a)
    a_ref[...] = a_split
    tf_ref[...] = mapped(a_split, jnp.where(later, gf, mf)) + jnp.where(later, mf, gf)
    x = jnp.where(later, bw, gw)
    joined = times(x, jnp.where(later, gw, aw))
    x_split = split_cols(x)
    x_ref[...] = x_split
    sums = mapped(x_split, jnp.where(later, gf, af)) + jnp.where(later, bf, gf)
    nbw_ref[...] = jnp.where(later, joined, bw)
    nbf_ref[...] = jnp.where(later, sums, bf)
    naw_ref[...] = jnp.where(later, aw, joined)
    naf_ref[...] = jnp.where(later, af, sums)


def again_first_kernel(distance, mf_ref, gf_ref, a_ref, tf_ref, bf_ref, af_ref):
    later = is_later(distance)
    mf, gf = mf_ref[...], gf_ref[...]
    tf_ref[...] = mapped(a_ref[...], jnp.where(later, gf, mf)) + jnp.where(later, mf, gf)
    bf_ref[...] = jnp.where(later, gf, 0.0)
    af_ref[...] = jnp.where(later, 0.0, gf)


def again_next_kernel(
    distance, mf_ref, gf_ref, bf_ref, af_ref, a_ref, x_ref, tf_ref, nbf_ref, naf_ref
):
    later = is_later(distance)
    mf, gf, bf, af = mf_ref[...], gf_ref[...], bf_ref[...], af_ref[...]
    tf_ref[...] = mapped(a_ref[...], jnp.where(later, gf, mf)) + jnp.where(later, mf, gf)
    sums = mapped(x_ref[...], jnp.where(later, gf, af)) + jnp.where(later, bf, gf)
    nbf_ref[...] = jnp.where(later, sums, bf)
    naf_ref[...] = jnp.where(later, af, sums)


def incoming(tail, maps, sums):
    for matrix, vector in zip(maps, sums):
        tail = mapped(matrix, tail) + vector[:1]
    return tail


def turn_kernel(
    tail_ref, aws_ref, af_ref, gws_ref, gf_ref, bws_ref, bf_ref, ps_ref, x_ref, s_ref,
    halo_ref, inj_ref, cap_ref, gain_ref, gs_ref, ds_ref, bnd_ref,
    new_s_ref, new_halo_ref, nr_ref, c_ref, msg_ref,
):
    points = s_ref.shape[0]
    came = incoming(
        tail_ref[...],
        (aws_ref[...], gws_ref[...], bws_ref[...]),
        (af_ref[...], gf_ref[...], bf_ref[...]),
    )
    s = s_ref[...] + x_ref[...] + mapped_each(ps_ref[...], came[:points])
    halo = halo_ref[...] + came[points : points + 1]
    new_s_ref[...] = s
    new_halo_ref[...] = halo
    first_half_of_step(
        s, halo, inj_ref[...], cap_ref[...], gain_ref[...],
        gs_ref, ds_ref, bnd_ref, nr_ref, c_ref, msg_ref,
    )


def end_kernel(
    tail_ref, aws_ref, af_ref, gws_ref, gf_ref, bws_ref, bf_ref, ps_ref, x_ref, s_ref, new_s_ref
):
    points = s_ref.shape[0]
    came = incoming(
        tail_ref[...],
        (aws_ref[...], gws_ref[...], bws_ref[...]),
        (af_ref[...], gf_ref[...], bf_ref[...]),
    )
    new_s_ref[...] = s_ref[...] + x_ref[...] + mapped_each(ps_ref[...], came[:points])


def splits_kernel(a_ref, b_ref, c_ref, as_ref, bs_ref, cs_ref):
    as_ref[...] = split_cols(a_ref[...])
    bs_ref[...] = split_cols(b_ref[...])
    cs_ref[...] = split_cols(c_ref[...])


def exchanged(value, distance):
    devices = range(lax.axis_size("tm"))
    return jax.tree.map(lambda v: lax.ppermute(v, "tm", [(i, i ^ distance) for i in devices]), value)


def handed_on(message, place):
    count = lax.axis_size("dom")
    pairs = []
    for i in range(0, count, 2):
        a, b = (i + place - 1) % count, (i + place) % count
        pairs += [(a, b), (b, a)]
    return lax.ppermute(message, "dom", pairs)


def per_device(
    starting_voltage_guess,
    injected_amperes,
    capacitance,
    conductance,
    block_pattern,
    device_gain,
    link_weight,
    boundary_vertex_list,
    diagonal_reciprocals,
    boundary_jacobian,
    transfer,
):
    points, _, width = starting_voltage_guess.shape
    segments, parts = lax.axis_size("tm"), lax.axis_size("dom")
    s = starting_voltage_guess[:, 0]
    inj = injected_amperes[:, 0]
    r = transfer[:, 0, 0]
    d = diagonal_reciprocals[:, 0, 0]
    cap, gain, bnd = capacitance, device_gain, boundary_vertex_list
    vec, eight, square = ((points, width), F32), ((8, width), F32), ((width, width), F32)
    square_split = ((width, 2 * width), BF16)
    many_split = ((points * width, 2 * width), BF16)
    one = ((1, width), F32)
    msg_shape = ((2 * points, width), F32)

    halo = lax.ppermute(
        s[points - 1 :], "tm", [(i, (i + 1) % segments) for i in range(segments)]
    )
    ds, js, ks, gs = call(
        prepare_kernel, [many_split] + [square_split] * 3,
        d, boundary_jacobian[0], link_weight[0], conductance[0], block_pattern[0],
    )
    ss, w = call(suffix_kernel, [many_split, square], r)
    levels = points.bit_length() - 1
    ps, ls = call(
        prefix_kernel, [many_split, ((levels * points // 2 * width, 2 * width), BF16)], r
    )
    nr, c, msg = call(start_kernel, [vec, vec, msg_shape], halo, s, inj, cap, gain, gs, ds, bnd)
    distances = [2**k for k in range(segments.bit_length() - 1)]
    kept = {}
    for step in range(ITERS):
        for place in range(1, parts):
            got = handed_on(msg, place)
            if place < parts - 1:
                c, msg = call(
                    functools.partial(hop_kernel, place), [vec, msg_shape],
                    got, c, msg, nr, ds, js, ks, bnd,
                )
        c, tail, f = call(
            functools.partial(last_hop_kernel, parts - 1),
            [vec, ((points + 8, width), F32), eight],
            got, c, nr, ds, js, ks, ss,
        )
        (x,) = call(scan_kernel, [vec], c, ls)
        for level, distance in enumerate(distances):
            last = level == len(distances) - 1
            if step == 0:
                both = exchanged(jnp.concatenate([w, f], axis=0), distance)
                gw, gf = both[:width], both[width:]
                if last:
                    kept["maps"] = call(splits_kernel, [square_split] * 3, aw, gw, bw)
                elif level == 0:
                    w, f, kept["a", 0], bw, bf, aw, af = call(
                        functools.partial(first_level_kernel, distance),
                        [square, eight, square_split, square, eight, square, eight],
                        w, f, gw, gf,
                    )
                else:
                    w, f, kept["a", level], kept["x", level], bw, bf, aw, af = call(
                        functools.partial(next_level_kernel, distance),
                        [square, eight, square_split, square_split, square, eight, square, eight],
                        w, f, gw, gf, bw, bf, aw, af,
                    )
            else:
                gf = exchanged(f, distance)
                if last:
                    pass
                elif level == 0:
                    f, bf, af = call(
                        functools.partial(again_first_kernel, distance), [eight] * 3,
                        f, gf, kept["a", 0],
                    )
                else:
                    f, bf, af = call(
                        functools.partial(again_next_kernel, distance), [eight] * 3,
                        f, gf, bf, af, kept["a", level], kept["x", level],
                    )
        aws, gws, bws = kept["maps"]
        ring = (tail, aws, af, gws, gf, bws, bf, ps, x, s)
        if step < ITERS - 1:
            s, halo, nr, c, msg = call(
                turn_kernel, [vec, one, vec, vec, msg_shape],
                *ring, halo, inj, cap, gain, gs, ds, bnd,
            )
        else:
            (s,) = call(end_kernel, [vec], *ring)
    return s[:, None]


def solution(mesh):
    in_specs = (
        P("tm", "dom", None),
        P("tm", "dom", None),
        P("dom", None),
        P("dom", None, None),
        P("dom", None, None),
        P("dom", None),
        P("dom", None, None),
        P("dom", None),
        P("tm", "dom", None, None, None),
        P("dom", None, None),
        P("tm", "dom", None, None, None),
    )
    out_specs = P("tm", "dom", None)
    return jax.shard_map(
        per_device, mesh=mesh, in_specs=in_specs, out_specs=out_specs, check_vma=False
    )
```

profile of v0, /device:TPU:0, one launch (start us, length us, event | category | flops | bytes accessed | tf_op | source)
XLA Modules:
  0.0 56.3 jit_solution(17491014255801804197)
XLA Ops:
  0.7 3.0 %collective-permute-start = (f32[1,128]{1,0:T(1,128)S(1)}, f32[1,128]{1,0:T(1,128)S(1)}, u32[]{:S(2)}, u32[]{:S(2)}) collective-permute-start(f32[1,128]{1,0:T(1,128)S(1)} %slice_bitcast_fusion), channel_id=1, source_target_pairs={{0,4},{4,8},{8,12},{12,16},{16,20},{20,24},{24,28},{28,0},{1,5},{5... | collective-permute-start | bytes 1544 | tf_op jit(solution)/shard_map/ppermute | solution.py:373
  4.3 1.2 %copy-done.1 = f32[16,1,1,128,128]{4,3,2,1,0:T(8,128)S(1)} copy-done((f32[16,1,1,128,128]{4,3,2,1,0:T(8,128)S(1)}, f32[16,1,1,128,128]{4,3,2,1,0:T(8,128)}, u32[]{:S(2)}) %copy-start.1) | copy-done | bytes 1048600
  5.5 0.8 %copy-done.2 = f32[1,128,128]{2,1,0:T(8,128)S(1)} copy-done((f32[1,128,128]{2,1,0:T(8,128)S(1)}, f32[1,128,128]{2,1,0:T(8,128)}, u32[]{:S(2)}) %copy-start.2) | copy-done | bytes 65560
  6.3 0.8 %copy-done.3 = f32[1,128,128]{2,1,0:T(8,128)S(1)} copy-done((f32[1,128,128]{2,1,0:T(8,128)S(1)}, f32[1,128,128]{2,1,0:T(8,128)}, u32[]{:S(2)}) %copy-start.3) | copy-done | bytes 65560
  7.2 0.8 %copy-done.4 = f32[1,128,128]{2,1,0:T(8,128)S(1)} copy-done((f32[1,128,128]{2,1,0:T(8,128)S(1)}, f32[1,128,128]{2,1,0:T(8,128)}, u32[]{:S(2)}) %copy-start.4) | copy-done | bytes 65560
  8.2 0.8 %copy-done.5 = f32[16,1,128]{2,1,0:T(1,128)S(1)} copy-done((f32[16,1,128]{2,1,0:T(1,128)S(1)}, f32[16,1,128]{2,1,0:T(1,128)}, u32[]{:S(2)}) %copy-start.5) | copy-done | bytes 8216
  9.0 0.7 %copy-done.6 = f32[16,1,128]{2,1,0:T(1,128)S(1)} copy-done((f32[16,1,128]{2,1,0:T(1,128)S(1)}, f32[16,1,128]{2,1,0:T(1,128)}, u32[]{:S(2)}) %copy-start.6) | copy-done | bytes 8216
  11.7 0.7 %shard_map.110 = (f32[16,128]{1,0:T(8,128)S(1)}, f32[16,128]{1,0:T(8,128)S(1)}, f32[32,128]{1,0:T(8,128)S(1)}) custom-call(f32[1,128]{1,0:T(1,128)S(1)} %collective-permute-done.halo_ref, f32[16,128]{1,0:T(8,128)S(1)} %bitcast.20, f32[16,128]{1,0:T(8,128)S(1)} %bitcast.22, f32[1,128]{1,0:T(1,128)S(1)} %copy-done.8, f32[1,128]{1,0:T(1,128)S(1)} %copy-done.10, ...), custom_call_target="tpu_custom_call" | custom-call | tf_op jit(solution)/shard_map/pallas_call | solution.py:63
  12.4 1.2 %collective-permute-done.1.got_ref = f32[32,128]{1,0:T(8,128)S(1)} collective-permute-done((f32[32,128]{1,0:T(8,128)S(1)}, f32[32,128]{1,0:T(8,128)S(1)}, u32[]{:S(2)}, u32[]{:S(2)}) %collective-permute-start.1) | collective-permute-done | bytes 16416 | tf_op jit(solution)/shard_map/ppermute | solution.py:344
  13.6 1.4 %collective-permute-start.2 = (f32[32,128]{1,0:T(8,128)S(1)}, f32[32,128]{1,0:T(8,128)S(1)}, u32[]{:S(2)}, u32[]{:S(2)}) collective-permute-start(f32[32,128]{1,0:T(8,128)S(1)} %get-tuple-element.65.msg_ref), channel_id=1, source_target_pairs={{1,2},{2,1},{3,0},{0,3},{5,6},{6,5},{7,4},{4,7},{9,10},{10,9},{11,... | collective-permute-start | bytes 49160 | tf_op jit(solution)/shard_map/ppermute | solution.py:344
  14.9 1.8 %collective-permute-done.2.got_ref = f32[32,128]{1,0:T(8,128)S(1)} collective-permute-done((f32[32,128]{1,0:T(8,128)S(1)}, f32[32,128]{1,0:T(8,128)S(1)}, u32[]{:S(2)}, u32[]{:S(2)}) %collective-permute-start.2) | collective-permute-done | bytes 16416 | tf_op jit(solution)/shard_map/ppermute | solution.py:344
  16.7 0.9 %collective-permute-start.3 = (f32[32,128]{1,0:T(8,128)S(1)}, f32[32,128]{1,0:T(8,128)S(1)}, u32[]{:S(2)}, u32[]{:S(2)}) collective-permute-start(f32[32,128]{1,0:T(8,128)S(1)} %get-tuple-element.67), channel_id=1, source_target_pairs={{2,3},{3,2},{0,1},{1,0},{6,7},{7,6},{4,5},{5,4},{10,11},{11,10},{8... | collective-permute-start | bytes 49160 | tf_op jit(solution)/shard_map/ppermute | solution.py:344
  17.6 1.0 %shard_map.113 = (bf16[2048,256]{1,0:T(8,128)(2,1)S(1)}, f32[128,128]{1,0:T(8,128)S(1)}) custom-call(f32[16,128,128]{2,1,0:T(8,128)S(1)} %bitcast.14), custom_call_target="tpu_custom_call" | custom-call | tf_op jit(solution)/shard_map/pallas_call | solution.py:63
  19.1 1.6 %collective-permute-start.4 = (f32[136,128]{1,0:T(8,128)S(1)}, f32[136,128]{1,0:T(8,128)S(1)}, u32[]{:S(2)}, u32[]{:S(2)}) collective-permute-start(f32[136,128]{1,0:T(8,128)S(1)} %pad_maximum_fusion), channel_id=1, source_target_pairs={{0,4},{4,0},{8,12},{12,8},{16,20},{20,16},{24,28},{28,24},{1,5},{5... | collective-permute-start | bytes 208904 | tf_op jit(solution)/shard_map/ppermute | solution.py:335
  20.7 2.8 %collective-permute-done.4 = f32[136,128]{1,0:T(8,128)S(1)} collective-permute-done((f32[136,128]{1,0:T(8,128)S(1)}, f32[136,128]{1,0:T(8,128)S(1)}, u32[]{:S(2)}, u32[]{:S(2)}) %collective-permute-start.4) | collective-permute-done | bytes 69664 | tf_op jit(solution)/shard_map/ppermute | solution.py:335
  23.7 1.7 %collective-permute-start.5 = (f32[136,128]{1,0:T(8,128)S(1)}, f32[136,128]{1,0:T(8,128)S(1)}, u32[]{:S(2)}, u32[]{:S(2)}) collective-permute-start(f32[136,128]{1,0:T(8,128)S(1)} %pad_maximum_fusion.1), channel_id=1, source_target_pairs={{0,8},{4,12},{8,0},{12,4},{16,24},{20,28},{24,16},{28,20},{1,9},{5... | collective-permute-start | bytes 208904 | tf_op jit(solution)/shard_map/ppermute | solution.py:335
  25.4 2.7 %collective-permute-done.5 = f32[136,128]{1,0:T(8,128)S(1)} collective-permute-done((f32[136,128]{1,0:T(8,128)S(1)}, f32[136,128]{1,0:T(8,128)S(1)}, u32[]{:S(2)}, u32[]{:S(2)}) %collective-permute-start.5) | collective-permute-done | bytes 69664 | tf_op jit(solution)/shard_map/ppermute | solution.py:335
  28.4 2.7 %collective-permute-start.6 = (f32[136,128]{1,0:T(8,128)S(1)}, f32[136,128]{1,0:T(8,128)S(1)}, u32[]{:S(2)}, u32[]{:S(2)}) collective-permute-start(f32[136,128]{1,0:T(8,128)S(1)} %pad_maximum_fusion.2), channel_id=1, source_target_pairs={{0,16},{4,20},{8,24},{12,28},{16,0},{20,4},{24,8},{28,12},{1,17},{... | collective-permute-start | bytes 208904 | tf_op jit(solution)/shard_map/ppermute | solution.py:335
  31.0 1.2 %shard_map.118 = (bf16[2048,256]{1,0:T(8,128)(2,1)S(1)}, bf16[4096,256]{1,0:T(8,128)(2,1)S(1)}) custom-call(f32[16,128,128]{2,1,0:T(8,128)S(1)} %bitcast.15), custom_call_target="tpu_custom_call" | custom-call | tf_op jit(solution)/shard_map/pallas_call | solution.py:63
  32.2 1.8 %shard_map.119.x_ref = f32[16,128]{1,0:T(8,128)S(1)} custom-call(f32[16,128]{1,0:T(8,128)S(1)} %get-tuple-element.89.c_ref, bf16[4096,256]{1,0:T(8,128)(2,1)S(1)} %get-tuple-element.90.l_ref), custom_call_target="tpu_custom_call" | custom-call | tf_op jit(solution)/shard_map/pallas_call | solution.py:63
  34.1 2.0 %shard_map.120 = (f32[16,128]{1,0:T(8,128)S(1)}, f32[1,128]{1,0:T(1,128)}, f32[16,128]{1,0:T(8,128)S(1)}, f32[16,128]{1,0:T(8,128)S(1)}, f32[32,128]{1,0:T(8,128)S(1)}) custom-call(f32[24,128]{1,0:T(8,128)S(1)} %get-tuple-element.70.tail_ref, bf16[128,256]{1,0:T(8,128)(2,1)S(1)} %get-tuple-element.83.aws_ref, f32[8,128]{1,0:T(8,128)S(1)} %get-tuple-element.84.af_ref, ...), custom_call_target="tpu_custom_call" | custom-call | tf_op jit(solution)/shard_map/pallas_call | solution.py:63
  36.1 1.2 %collective-permute-done.7.got_ref = f32[32,128]{1,0:T(8,128)S(1)} collective-permute-done((f32[32,128]{1,0:T(8,128)S(1)}, f32[32,128]{1,0:T(8,128)S(1)}, u32[]{:S(2)}, u32[]{:S(2)}) %collective-permute-start.7) | collective-permute-done | bytes 16416 | tf_op jit(solution)/shard_map/ppermute | solution.py:344
  37.3 2.0 %collective-permute-start.8 = (f32[32,128]{1,0:T(8,128)S(1)}, f32[32,128]{1,0:T(8,128)S(1)}, u32[]{:S(2)}, u32[]{:S(2)}) collective-permute-start(f32[32,128]{1,0:T(8,128)S(1)} %get-tuple-element.94.msg_ref), channel_id=1, source_target_pairs={{1,2},{2,1},{3,0},{0,3},{5,6},{6,5},{7,4},{4,7},{9,10},{10,9},{11,... | collective-permute-start | bytes 49160 | tf_op jit(solution)/shard_map/ppermute | solution.py:344
  39.3 1.4 %collective-permute-done.8.got_ref = f32[32,128]{1,0:T(8,128)S(1)} collective-permute-done((f32[32,128]{1,0:T(8,128)S(1)}, f32[32,128]{1,0:T(8,128)S(1)}, u32[]{:S(2)}, u32[]{:S(2)}) %collective-permute-start.8) | collective-permute-done | bytes 16416 | tf_op jit(solution)/shard_map/ppermute | solution.py:344
  41.4 0.8 %collective-permute-done.9.got_ref = f32[32,128]{1,0:T(8,128)S(1)} collective-permute-done((f32[32,128]{1,0:T(8,128)S(1)}, f32[32,128]{1,0:T(8,128)S(1)}, u32[]{:S(2)}, u32[]{:S(2)}) %collective-permute-start.9) | collective-permute-done | bytes 16416 | tf_op jit(solution)/shard_map/ppermute | solution.py:344
  42.7 1.6 %collective-permute-start.10 = (f32[8,128]{1,0:T(8,128)S(1)}, f32[8,128]{1,0:T(8,128)S(1)}, u32[]{:S(2)}, u32[]{:S(2)}) collective-permute-start(f32[8,128]{1,0:T(8,128)S(1)} %get-tuple-element.99.mf_ref), channel_id=1, source_target_pairs={{0,4},{4,0},{8,12},{12,8},{16,20},{20,16},{24,28},{28,24},{1,5},{5... | collective-permute-start | bytes 12296 | tf_op jit(solution)/shard_map/ppermute | solution.py:335
  44.3 2.1 %collective-permute-done.10.gf_ref = f32[8,128]{1,0:T(8,128)S(1)} collective-permute-done((f32[8,128]{1,0:T(8,128)S(1)}, f32[8,128]{1,0:T(8,128)S(1)}, u32[]{:S(2)}, u32[]{:S(2)}) %collective-permute-start.10) | collective-permute-done | bytes 4128 | tf_op jit(solution)/shard_map/ppermute | solution.py:335
  46.5 1.6 %collective-permute-start.11 = (f32[8,128]{1,0:T(8,128)S(1)}, f32[8,128]{1,0:T(8,128)S(1)}, u32[]{:S(2)}, u32[]{:S(2)}) collective-permute-start(f32[8,128]{1,0:T(8,128)S(1)} %get-tuple-element.101.mf_ref), channel_id=1, source_target_pairs={{0,8},{4,12},{8,0},{12,4},{16,24},{20,28},{24,16},{28,20},{1,9},{5... | collective-permute-start | bytes 12296 | tf_op jit(solution)/shard_map/ppermute | solution.py:335
  48.1 2.0 %collective-permute-done.11.gf_ref = f32[8,128]{1,0:T(8,128)S(1)} collective-permute-done((f32[8,128]{1,0:T(8,128)S(1)}, f32[8,128]{1,0:T(8,128)S(1)}, u32[]{:S(2)}, u32[]{:S(2)}) %collective-permute-start.11) | collective-permute-done | bytes 4128 | tf_op jit(solution)/shard_map/ppermute | solution.py:335
  50.3 2.4 %collective-permute-start.12 = (f32[8,128]{1,0:T(8,128)S(1)}, f32[8,128]{1,0:T(8,128)S(1)}, u32[]{:S(2)}, u32[]{:S(2)}) collective-permute-start(f32[8,128]{1,0:T(8,128)S(1)} %get-tuple-element.107), channel_id=1, source_target_pairs={{0,16},{4,20},{8,24},{12,28},{16,0},{20,4},{24,8},{28,12},{1,17},{... | collective-permute-start | bytes 12296 | tf_op jit(solution)/shard_map/ppermute | solution.py:335
  52.7 1.8 %shard_map.126.x_ref = f32[16,128]{1,0:T(8,128)S(1)} custom-call(f32[16,128]{1,0:T(8,128)S(1)} %get-tuple-element.109.c_ref, bf16[4096,256]{1,0:T(8,128)(2,1)S(1)} %get-tuple-element.90.l_ref), custom_call_target="tpu_custom_call" | custom-call | tf_op jit(solution)/shard_map/pallas_call | solution.py:63
  54.8 1.5 %shard_map.127 = f32[16,128]{1,0:T(8,128)} custom-call(f32[24,128]{1,0:T(8,128)S(1)} %get-tuple-element.98.tail_ref, bf16[128,256]{1,0:T(8,128)(2,1)S(1)} %get-tuple-element.83.aws_ref, f32[8,128]{1,0:T(8,128)S(1)} %get-tuple-element.106.af_ref, bf16[128,256]{1,0:T(8,128)(2,1)S(1)} %get-tuple-element.85.gws_ref, ...), custom_call_target="tpu_custom_call" | custom-call | tf_op jit(solution)/shard_map/pallas_call | solution.py:63
  (47 shorter events, 5.6 us)
Async XLA Ops:
  0.7 7.5 %collective-permute-start = (f32[1,128]{1,0:T(1,128)S(1)}, f32[1,128]{1,0:T(1,128)S(1)}, u32[]{:S(2)}, u32[]{:S(2)}) collective-permute-start(f32[1,128]{1,0:T(1,128)S(1)} %slice_bitcast_fusion), channel_id=1, source_target_pairs={{0,4},{4,8},{8,12},{12,16},{16,20},{20,24},{24,28},{28,0},{1,5},{5... | collective-permute-start | bytes 1544 | tf_op jit(solution)/shard_map/ppermute | solution.py:373
  4.3 1.2 %copy-start.1 = (f32[16,1,1,128,128]{4,3,2,1,0:T(8,128)S(1)}, f32[16,1,1,128,128]{4,3,2,1,0:T(8,128)}, u32[]{:S(2)}) copy-start(f32[16,1,1,128,128]{4,3,2,1,0:T(8,128)} %param.19) | copy-start | bytes 3145732
  5.5 0.8 %copy-start.2 = (f32[1,128,128]{2,1,0:T(8,128)S(1)}, f32[1,128,128]{2,1,0:T(8,128)}, u32[]{:S(2)}) copy-start(f32[1,128,128]{2,1,0:T(8,128)} %param.20) | copy-start | bytes 196612
  6.3 0.8 %copy-start.3 = (f32[1,128,128]{2,1,0:T(8,128)S(1)}, f32[1,128,128]{2,1,0:T(8,128)}, u32[]{:S(2)}) copy-start(f32[1,128,128]{2,1,0:T(8,128)} %param.17) | copy-start | bytes 196612
  7.2 0.8 %copy-start.4 = (f32[1,128,128]{2,1,0:T(8,128)S(1)}, f32[1,128,128]{2,1,0:T(8,128)}, u32[]{:S(2)}) copy-start(f32[1,128,128]{2,1,0:T(8,128)} %param.14) | copy-start | bytes 196612
  8.2 9.4 %copy-start = (f32[16,1,1,128,128]{4,3,2,1,0:T(8,128)S(1)}, f32[16,1,1,128,128]{4,3,2,1,0:T(8,128)}, u32[]{:S(2)}) copy-start(f32[16,1,1,128,128]{4,3,2,1,0:T(8,128)} %param.21) | copy-start | bytes 3145732
  8.2 0.8 %copy-start.5 = (f32[16,1,128]{2,1,0:T(1,128)S(1)}, f32[16,1,128]{2,1,0:T(1,128)}, u32[]{:S(2)}) copy-start(f32[16,1,128]{2,1,0:T(1,128)} %param.11) | copy-start | bytes 24580
  9.0 0.7 %copy-start.6 = (f32[16,1,128]{2,1,0:T(1,128)S(1)}, f32[16,1,128]{2,1,0:T(1,128)}, u32[]{:S(2)}) copy-start(f32[16,1,128]{2,1,0:T(1,128)} %param.12) | copy-start | bytes 24580
  9.7 0.7 %copy-start.7 = (s32[1,128]{1,0:T(1,128)S(1)}, s32[1,128]{1,0:T(1,128)}, u32[]{:S(2)}) copy-start(s32[1,128]{1,0:T(1,128)} %bnd_ref.11) | copy-start | bytes 1540
  10.3 0.7 %copy-start.8 = (f32[1,128]{1,0:T(1,128)S(1)}, f32[1,128]{1,0:T(1,128)}, u32[]{:S(2)}) copy-start(f32[1,128]{1,0:T(1,128)} %cap_ref.3) | copy-start | bytes 1540
  11.0 0.7 %copy-start.10 = (f32[1,128]{1,0:T(1,128)S(1)}, f32[1,128]{1,0:T(1,128)}, u32[]{:S(2)}) copy-start(f32[1,128]{1,0:T(1,128)} %gain_ref.3) | copy-start | bytes 1540
  12.3 1.2 %collective-permute-start.1 = (f32[32,128]{1,0:T(8,128)S(1)}, f32[32,128]{1,0:T(8,128)S(1)}, u32[]{:S(2)}, u32[]{:S(2)}) collective-permute-start(f32[32,128]{1,0:T(8,128)S(1)} %get-tuple-element.60.msg_ref), channel_id=1, source_target_pairs={{0,1},{1,0},{2,3},{3,2},{4,5},{5,4},{6,7},{7,6},{8,9},{9,8},{10,11... | collective-permute-start | bytes 49160 | tf_op jit(solution)/shard_map/ppermute | solution.py:344
  13.6 3.2 %collective-permute-start.2 = (f32[32,128]{1,0:T(8,128)S(1)}, f32[32,128]{1,0:T(8,128)S(1)}, u32[]{:S(2)}, u32[]{:S(2)}) collective-permute-start(f32[32,128]{1,0:T(8,128)S(1)} %get-tuple-element.65.msg_ref), channel_id=1, source_target_pairs={{1,2},{2,1},{3,0},{0,3},{5,6},{6,5},{7,4},{4,7},{9,10},{10,9},{11,... | collective-permute-start | bytes 49160 | tf_op jit(solution)/shard_map/ppermute | solution.py:344
  16.7 1.9 %collective-permute-start.3 = (f32[32,128]{1,0:T(8,128)S(1)}, f32[32,128]{1,0:T(8,128)S(1)}, u32[]{:S(2)}, u32[]{:S(2)}) collective-permute-start(f32[32,128]{1,0:T(8,128)S(1)} %get-tuple-element.67), channel_id=1, source_target_pairs={{2,3},{3,2},{0,1},{1,0},{6,7},{7,6},{4,5},{5,4},{10,11},{11,10},{8... | collective-permute-start | bytes 49160 | tf_op jit(solution)/shard_map/ppermute | solution.py:344
  19.1 4.4 %collective-permute-start.4 = (f32[136,128]{1,0:T(8,128)S(1)}, f32[136,128]{1,0:T(8,128)S(1)}, u32[]{:S(2)}, u32[]{:S(2)}) collective-permute-start(f32[136,128]{1,0:T(8,128)S(1)} %pad_maximum_fusion), channel_id=1, source_target_pairs={{0,4},{4,0},{8,12},{12,8},{16,20},{20,16},{24,28},{28,24},{1,5},{5... | collective-permute-start | bytes 208904 | tf_op jit(solution)/shard_map/ppermute | solution.py:335
  23.7 10.4 %copy-start.9 = (f32[1,128]{1,0:T(1,128)S(1)}, f32[1,128]{1,0:T(1,128)}, u32[]{:S(2)}) copy-start(f32[1,128]{1,0:T(1,128)} %cap_ref.3) | copy-start | bytes 1540
  23.7 10.4 %copy-start.11 = (f32[1,128]{1,0:T(1,128)S(1)}, f32[1,128]{1,0:T(1,128)}, u32[]{:S(2)}) copy-start(f32[1,128]{1,0:T(1,128)} %gain_ref.3) | copy-start | bytes 1540
  23.7 4.4 %collective-permute-start.5 = (f32[136,128]{1,0:T(8,128)S(1)}, f32[136,128]{1,0:T(8,128)S(1)}, u32[]{:S(2)}, u32[]{:S(2)}) collective-permute-start(f32[136,128]{1,0:T(8,128)S(1)} %pad_maximum_fusion.1), channel_id=1, source_target_pairs={{0,8},{4,12},{8,0},{12,4},{16,24},{20,28},{24,16},{28,20},{1,9},{5... | collective-permute-start | bytes 208904 | tf_op jit(solution)/shard_map/ppermute | solution.py:335
  28.4 5.6 %collective-permute-start.6 = (f32[136,128]{1,0:T(8,128)S(1)}, f32[136,128]{1,0:T(8,128)S(1)}, u32[]{:S(2)}, u32[]{:S(2)}) collective-permute-start(f32[136,128]{1,0:T(8,128)S(1)} %pad_maximum_fusion.2), channel_id=1, source_target_pairs={{0,16},{4,20},{8,24},{12,28},{16,0},{20,4},{24,8},{28,12},{1,17},{... | collective-permute-start | bytes 208904 | tf_op jit(solution)/shard_map/ppermute | solution.py:335
  36.1 1.2 %collective-permute-start.7 = (f32[32,128]{1,0:T(8,128)S(1)}, f32[32,128]{1,0:T(8,128)S(1)}, u32[]{:S(2)}, u32[]{:S(2)}) collective-permute-start(f32[32,128]{1,0:T(8,128)S(1)} %get-tuple-element.91.msg_ref), channel_id=1, source_target_pairs={{0,1},{1,0},{2,3},{3,2},{4,5},{5,4},{6,7},{7,6},{8,9},{9,8},{10,11... | collective-permute-start | bytes 49160 | tf_op jit(solution)/shard_map/ppermute | solution.py:344
  37.3 3.4 %collective-permute-start.8 = (f32[32,128]{1,0:T(8,128)S(1)}, f32[32,128]{1,0:T(8,128)S(1)}, u32[]{:S(2)}, u32[]{:S(2)}) collective-permute-start(f32[32,128]{1,0:T(8,128)S(1)} %get-tuple-element.94.msg_ref), channel_id=1, source_target_pairs={{1,2},{2,1},{3,0},{0,3},{5,6},{6,5},{7,4},{4,7},{9,10},{10,9},{11,... | collective-permute-start | bytes 49160 | tf_op jit(solution)/shard_map/ppermute | solution.py:344
  40.7 1.5 %collective-permute-start.9 = (f32[32,128]{1,0:T(8,128)S(1)}, f32[32,128]{1,0:T(8,128)S(1)}, u32[]{:S(2)}, u32[]{:S(2)}) collective-permute-start(f32[32,128]{1,0:T(8,128)S(1)} %get-tuple-element.96), channel_id=1, source_target_pairs={{2,3},{3,2},{0,1},{1,0},{6,7},{7,6},{4,5},{5,4},{10,11},{11,10},{8... | collective-permute-start | bytes 49160 | tf_op jit(solution)/shard_map/ppermute | solution.py:344
  42.7 3.7 %collective-permute-start.10 = (f32[8,128]{1,0:T(8,128)S(1)}, f32[8,128]{1,0:T(8,128)S(1)}, u32[]{:S(2)}, u32[]{:S(2)}) collective-permute-start(f32[8,128]{1,0:T(8,128)S(1)} %get-tuple-element.99.mf_ref), channel_id=1, source_target_pairs={{0,4},{4,0},{8,12},{12,8},{16,20},{20,16},{24,28},{28,24},{1,5},{5... | collective-permute-start | bytes 12296 | tf_op jit(solution)/shard_map/ppermute | solution.py:335
  46.5 3.6 %collective-permute-start.11 = (f32[8,128]{1,0:T(8,128)S(1)}, f32[8,128]{1,0:T(8,128)S(1)}, u32[]{:S(2)}, u32[]{:S(2)}) collective-permute-start(f32[8,128]{1,0:T(8,128)S(1)} %get-tuple-element.101.mf_ref), channel_id=1, source_target_pairs={{0,8},{4,12},{8,0},{12,4},{16,24},{20,28},{24,16},{28,20},{1,9},{5... | collective-permute-start | bytes 12296 | tf_op jit(solution)/shard_map/ppermute | solution.py:335
  50.3 4.5 %collective-permute-start.12 = (f32[8,128]{1,0:T(8,128)S(1)}, f32[8,128]{1,0:T(8,128)S(1)}, u32[]{:S(2)}, u32[]{:S(2)}) collective-permute-start(f32[8,128]{1,0:T(8,128)S(1)} %get-tuple-element.107), channel_id=1, source_target_pairs={{0,16},{4,20},{8,24},{12,28},{16,0},{20,4},{24,8},{28,12},{1,17},{... | collective-permute-start | bytes 12296 | tf_op jit(solution)/shard_map/ppermute | solution.py:335
where the time goes:
time: 56.6 us; the launch traced here: 56.3 us
  starting transfers between devices  19.5 us (34%)
  waiting for transfers between devices  16.3 us (29%)
  Pallas kernels  11.7 us (21%)
  local copies, waits for them, and re-layouts  7.87 us (14%)
  between operations  0.87 us (2%)
    pallas_call x19, Pallas kernels, call(): pl.pallas_call(kernel, out_shape=[jax.ShapeDtypeStruct(s, d) for s, d in...  11.7 us
    ppermute x6, starting transfers between devices, exchanged(): lax.ppermute(v, 'tm', [(i, i ^ distance) for i in devices])  11.6 us
    ppermute x6, waiting for transfers between devices, exchanged(): lax.ppermute(v, 'tm', [(i, i ^ distance) for i in devices])  9.89 us
    unnamed x24, local copies, waits for them, and re-layouts  7.19 us
    ppermute x6, waiting for transfers between devices, handed_on(): return lax.ppermute(message, 'dom', pairs)  6.43 us
    ppermute x6, starting transfers between devices, handed_on(): return lax.ppermute(message, 'dom', pairs)  4.98 us
    ppermute x1, starting transfers between devices, per_device(): lax.ppermute(s[points - 1:], 'tm', [(i, (i + 1) % segments) for i in rang...  2.97 us
  transfers between devices with their start and end apart: 13, of which 10 were waited for; matrix products, arithmetic and copies ran while one was open for 0% of the time, Pallas kernels for 10%

commit v1 on v0

v1 whole, which is shorter than its diff:
```python
import functools

import jax
import jax.numpy as jnp
from jax import lax
from jax.experimental import pallas as pl
from jax.experimental.pallas import tpu as pltpu
from jax.sharding import PartitionSpec as P

ITERS = 2
F32 = jnp.float32
BF16 = jnp.bfloat16


def halves(x):
    hi = x.astype(BF16)
    return hi, (x - hi.astype(F32)).astype(BF16)


def split_cols(matrix):
    return jnp.concatenate(halves(matrix), axis=1)


def split_rows(vectors):
    hi, lo = halves(vectors)
    hi, lo = hi.astype(F32), lo.astype(F32)
    top = jnp.concatenate([hi, hi], axis=1)
    low = jnp.concatenate([lo, jnp.zeros_like(lo)], axis=1)
    return jnp.concatenate([top, low], axis=0).astype(BF16)


def dot_nt(a, b):
    return lax.dot_general(a, b, (((1,), (1,)), ((), ())), preferred_element_type=F32)


def times(a, b):
    ah, al = halves(a)
    bh, bl = halves(b)
    left = jnp.concatenate([ah, al, ah], axis=1)
    right = jnp.concatenate([bh, bh, bl], axis=0)
    return jnp.dot(left, right, preferred_element_type=F32)


def mapped(matrix_split, vectors):
    count = vectors.shape[0]
    both = dot_nt(split_rows(vectors), matrix_split)
    return both[:count] + both[count:]


def mapped_each(matrices, vectors):
    rows = []
    for r in range(vectors.shape[0]):
        products = matrices[r] * vectors[r : r + 1, :]
        rows.append(jnp.sum(products.T, axis=0, keepdims=True))
    return jnp.concatenate(rows, axis=0)


def call(kernel, outs, *args, source=pltpu.VMEM, scratch=(), cost=None):
    return pl.pallas_call(
        kernel,
        out_shape=[jax.ShapeDtypeStruct(s, d) for s, d in outs],
        in_specs=[pl.BlockSpec(memory_space=source)] * len(args),
        out_specs=[pl.BlockSpec(memory_space=pltpu.VMEM)] * len(outs),
        scratch_shapes=list(scratch),
        cost_estimate=cost,
        compiler_params=pltpu.CompilerParams(vmem_limit_bytes=24 * 2**20),
    )(*args)


def identity(width):
    return (
        lax.broadcasted_iota(jnp.int32, (width, width), 0)
        == lax.broadcasted_iota(jnp.int32, (width, width), 1)
    ).astype(F32)


def identity_kernel(eye_ref):
    eye_ref[...] = identity(eye_ref.shape[0])


def suffix_products(r_ref, eye, s_ref, w_ref):
    points, width = r_ref.shape[0], r_ref.shape[1]
    u = [r_ref[i] for i in range(points)]
    span = 1
    while span < points:
        for base in range(0, points, 2 * span):
            mid = u[base + span]
            prod = times(mid, jnp.concatenate(u[base : base + span], axis=1))
            for i in range(span):
                u[base + i] = prod[:, i * width : (i + 1) * width]
        span *= 2
    w_ref[...] = u[0]
    for i in range(points - 1):
        s_ref[i] = u[i + 1]
    s_ref[points - 1] = eye


def prefix_products(r_ref, p_ref, l_ref):
    points, width = r_ref.shape[0], r_ref.shape[1]
    q = [r_ref[i] for i in range(points)]
    span, slot = 1, 0
    while span < points:
        for base in range(0, points, 2 * span):
            upper = q[base + span : base + 2 * span]
            for matrix in upper:
                l_ref[slot] = matrix
                slot += 1
            prod = times(jnp.concatenate(upper, axis=0), q[base + span - 1])
            for i in range(span):
                q[base + span + i] = prod[i * width : (i + 1) * width]
        span *= 2
    for i in range(points):
        p_ref[i] = q[i]


def scanned(c, l_ref):
    points = c.shape[0]
    half = points // 2
    x = [c[i : i + 1, :] for i in range(points)]
    span, level = 1, 0
    while span < points:
        slot = level * half
        for base in range(0, points, 2 * span):
            head = x[base + span - 1]
            for i in range(base + span, base + 2 * span):
                x[i] = x[i] + mapped_each(l_ref[slot : slot + 1], head)
                slot += 1
        span *= 2
        level += 1
    return jnp.concatenate(x, axis=0)


def taken(rows, lanes):
    return jnp.take_along_axis(rows, jnp.broadcast_to(lanes, rows.shape), axis=1)


def negative_residual(s, before, inj, cap, gain, gs):
    return inj - cap * (s - before) - mapped(gs, s) - gain * jnp.tanh(s)


def load_kernel(
    eye, s, inj, cap, g, mask, gain, k, d, j, r,
    js, ks, gs, nr, c, ss, w, ps, ls,
):
    points, width = s.shape
    js[...] = split_cols(j[...])
    ks[...] = split_cols(k[...])
    gs[...] = split_cols(g[...] * mask[...].astype(F32))
    volts = s[...]
    before = jnp.concatenate([jnp.zeros((1, width), F32), volts[: points - 1]], axis=0)
    nr[...] = negative_residual(volts, before, inj[...], cap[...], gain[...], gs[...])
    suffix_products(r, eye[...], ss, w)
    prefix_products(r, ps, ls)
    c[...] = mapped_each(d, nr[...])


def start_kernel(
    halo_ref, s_ref, cap_ref, bnd_ref, d_ref, nr_ref, c_ref,
    halo_out_ref, new_nr_ref, new_c_ref, msg_ref,
):
    points = s_ref.shape[0]
    halo = halo_ref[points - 1 :]
    halo_out_ref[...] = halo
    extra = cap_ref[...] * halo
    new_nr_ref[...] = nr_ref[...]
    new_nr_ref[:1] = nr_ref[:1] + extra
    new_c_ref[...] = c_ref[...]
    new_c_ref[:1] = c_ref[:1] + mapped_each(d_ref[:1], extra)
    msg_ref[:points] = taken(new_c_ref[...], bnd_ref[...])
    msg_ref[points:] = taken(s_ref[...], bnd_ref[...])


def inflow_applied(got_ref, nr_ref, d_ref, js_ref, ks_ref):
    points = nr_ref.shape[0]
    got = got_ref[...]
    nr = nr_ref[...] + mapped(js_ref[...], got[:points]) + mapped(ks_ref[...], got[points:])
    return mapped_each(d_ref, nr)


def hop_kernel(
    place, got_ref, c_ref, msg_ref, nr_ref, d_ref, js_ref, ks_ref, bnd_ref, new_c_ref, new_msg_ref
):
    points = c_ref.shape[0]
    here = lax.axis_index("dom") == place
    new_msg_ref[points:] = msg_ref[points:]

    @pl.when(here)
    def _():
        c = inflow_applied(got_ref, nr_ref, d_ref, js_ref, ks_ref)
        new_c_ref[...] = c
        new_msg_ref[:points] = taken(c, bnd_ref[...])

    @pl.when(jnp.logical_not(here))
    def _():
        new_c_ref[...] = c_ref[...]
        new_msg_ref[:points] = msg_ref[:points]


def last_hop_kernel(
    place, got_ref, c_ref, nr_ref, d_ref, js_ref, ks_ref, ss_ref, new_c_ref, tail_ref, f_ref
):
    points, width = c_ref.shape
    here = lax.axis_index("dom") == place

    @pl.when(here)
    def _():
        new_c_ref[...] = inflow_applied(got_ref, nr_ref, d_ref, js_ref, ks_ref)

    @pl.when(jnp.logical_not(here))
    def _():
        new_c_ref[...] = c_ref[...]

    total = mapped_each(ss_ref, new_c_ref[...])
    shift = 1
    while shift < points:
        total = total + jnp.concatenate([total[shift:], jnp.zeros((shift, width), F32)], axis=0)
        shift *= 2
    tail_ref[:points] = jnp.concatenate([total[1:], jnp.zeros((1, width), F32)], axis=0)
    tail_ref[points:] = jnp.broadcast_to(total[:1], (8, width))
    f_ref[...] = jnp.broadcast_to(total[:1], (8, width))


def is_later(distance):
    return (lax.axis_index("tm") // distance) % 2 == 1


def first_level_kernel(
    distance, mw_ref, mf_ref, gw_ref, gf_ref,
    tw_ref, tf_ref, a_ref, bw_ref, bf_ref, aw_ref, af_ref,
):
    width = mw_ref.shape[0]
    later = is_later(distance)
    mw, mf, gw, gf = mw_ref[...], mf_ref[...], gw_ref[...], gf_ref[...]
    a = jnp.where(later, mw, gw)
    tw_ref[...] = times(a, jnp.where(later, gw, mw))
    a_split = split_cols(a)
    a_ref[...] = a_split
    tf_ref[...] = mapped(a_split, jnp.where(later, gf, mf)) + jnp.where(later, mf, gf)
    eye = identity(width)
    bw_ref[...] = jnp.where(later, gw, eye)
    bf_ref[...] = jnp.where(later, gf, 0.0)
    aw_ref[...] = jnp.where(later, eye, gw)
    af_ref[...] = jnp.where(later, 0.0, gf)


def next_level_kernel(
    distance, mw_ref, mf_ref, gw_ref, gf_ref, bw_ref, bf_ref, aw_ref, af_ref,
    tw_ref, tf_ref, a_ref, x_ref, nbw_ref, nbf_ref, naw_ref, naf_ref,
):
    later = is_later(distance)
    mw, mf, gw, gf = mw_ref[...], mf_ref[...], gw_ref[...], gf_ref[...]
    bw, bf, aw, af = bw_ref[...], bf_ref[...], aw_ref[...], af_ref[...]
    a = jnp.where(later, mw, gw)
    tw_ref[...] = times(a, jnp.where(later, gw, mw))
    a_split = split_cols(a)
    a_ref[...] = a_split
    tf_ref[...] = mapped(a_split, jnp.where(later, gf, mf)) + jnp.where(later, mf, gf)
    x = jnp.where(later, bw, gw)
    joined = times(x, jnp.where(later, gw, aw))
    x_split = split_cols(x)
    x_ref[...] = x_split
    sums = mapped(x_split, jnp.where(later, gf, af)) + jnp.where(later, bf, gf)
    nbw_ref[...] = jnp.where(later, joined, bw)
    nbf_ref[...] = jnp.where(later, sums, bf)
    naw_ref[...] = jnp.where(later, aw, joined)
    naf_ref[...] = jnp.where(later, af, sums)


def again_first_kernel(distance, mf_ref, gf_ref, a_ref, tf_ref, bf_ref, af_ref):
    later = is_later(distance)
    mf, gf = mf_ref[...], gf_ref[...]
    tf_ref[...] = mapped(a_ref[...], jnp.where(later, gf, mf)) + jnp.where(later, mf, gf)
    bf_ref[...] = jnp.where(later, gf, 0.0)
    af_ref[...] = jnp.where(later, 0.0, gf)


def again_next_kernel(
    distance, mf_ref, gf_ref, bf_ref, af_ref, a_ref, x_ref, tf_ref, nbf_ref, naf_ref
):
    later = is_later(distance)
    mf, gf, bf, af = mf_ref[...], gf_ref[...], bf_ref[...], af_ref[...]
    tf_ref[...] = mapped(a_ref[...], jnp.where(later, gf, mf)) + jnp.where(later, mf, gf)
    sums = mapped(x_ref[...], jnp.where(later, gf, af)) + jnp.where(later, bf, gf)
    nbf_ref[...] = jnp.where(later, sums, bf)
    naf_ref[...] = jnp.where(later, af, sums)


def local_kernel(c_ref, ls_ref, tail_ref, aw_ref, af_ref, s_ref, base_ref, v_ref):
    base_ref[...] = s_ref[...] + scanned(c_ref[...], ls_ref)
    v_ref[...] = mapped(split_cols(aw_ref[...]), tail_ref[...]) + af_ref[:1]


def turn_kernel(
    v_ref, got_ref, bw_ref, bf_ref, ps_ref, base_ref,
    halo_ref, inj_ref, cap_ref, gain_ref, gs_ref, d_ref, bnd_ref,
    new_s_ref, nr_ref, c_ref, msg_ref,
):
    points, width = base_ref.shape
    v = mapped(split_cols(got_ref[:width]), v_ref[...]) + got_ref[width : width + 1]
    v = mapped(split_cols(bw_ref[...]), v) + bf_ref[:1]
    s = base_ref[...] + mapped_each(ps_ref, v[:points])
    new_s_ref[...] = s
    before = jnp.concatenate([halo_ref[...] + v[points : points + 1], s[: points - 1]], axis=0)
    nr = negative_residual(s, before, inj_ref[...], cap_ref[...], gain_ref[...], gs_ref[...])
    c = mapped_each(d_ref, nr)
    nr_ref[...] = nr
    c_ref[...] = c
    msg_ref[:points] = taken(c, bnd_ref[...])
    msg_ref[points:] = taken(s, bnd_ref[...])


def last_local_kernel(
    c_ref, ls_ref, tail_ref, aw_ref, af_ref, gw_ref, bw_ref, bf_ref, ps_ref, s_ref, base_ref
):
    points, width = s_ref.shape
    v = mapped(split_cols(aw_ref[...]), tail_ref[:points]) + af_ref[:1]
    v = mapped(split_cols(gw_ref[:width]), v)
    v = mapped(split_cols(bw_ref[...]), v) + bf_ref[:1]
    base_ref[...] = s_ref[...] + scanned(c_ref[...], ls_ref) + mapped_each(ps_ref, v)


def end_kernel(gf_ref, bw_ref, ps_ref, base_ref, s_ref):
    points, width = base_ref.shape
    v = mapped(split_cols(bw_ref[...]), gf_ref[...])[:1]
    s_ref[...] = base_ref[...] + mapped_each(ps_ref, jnp.broadcast_to(v, (points, width)))


def exchanged(value, distance):
    devices = range(lax.axis_size("tm"))
    return jax.tree.map(lambda v: lax.ppermute(v, "tm", [(i, i ^ distance) for i in devices]), value)


def handed_on(message, place):
    count = lax.axis_size("dom")
    pairs = []
    for i in range(0, count, 2):
        a, b = (i + place - 1) % count, (i + place) % count
        pairs += [(a, b), (b, a)]
    return lax.ppermute(message, "dom", pairs)


def per_device(
    starting_voltage_guess,
    injected_amperes,
    capacitance,
    conductance,
    block_pattern,
    device_gain,
    link_weight,
    boundary_vertex_list,
    diagonal_reciprocals,
    boundary_jacobian,
    transfer,
):
    points, _, width = starting_voltage_guess.shape
    segments, parts = lax.axis_size("tm"), lax.axis_size("dom")
    vec, eight, square = ((points, width), F32), ((8, width), F32), ((width, width), F32)
    square_split = ((width, 2 * width), BF16)
    many = ((points, width, width), F32)
    one = ((1, width), F32)
    longer = ((points + 8, width), F32)
    msg_shape = ((2 * points, width), F32)
    levels = points.bit_length() - 1

    halo = lax.ppermute(
        starting_voltage_guess, "tm", [(i, (i + 1) % segments) for i in range(segments)]
    )
    s, inj = starting_voltage_guess[:, 0], injected_amperes[:, 0]
    cap, gain, bnd = capacitance, device_gain, boundary_vertex_list
    d = diagonal_reciprocals[:, 0, 0]
    (eye,) = call(
        identity_kernel, [square],
        cost=pl.CostEstimate(flops=2**33, bytes_accessed=2**25, transcendentals=0),
    )
    js, ks, gs, nr, c, ss, w, ps, ls = call(
        load_kernel,
        [square_split] * 3
        + [vec, vec, many, square, many, ((levels * points // 2, width, width), F32)],
        eye, s, inj, cap, conductance[0], block_pattern[0], gain, link_weight[0], d,
        boundary_jacobian[0], transfer[:, 0, 0],
    )
    halo, nr, c, msg = call(
        start_kernel, [one, vec, vec, msg_shape], halo[:, 0], s, cap, bnd, d, nr, c
    )
    distances = [2**k for k in range(segments.bit_length() - 1)]
    kept = {}
    for step in range(ITERS):
        for place in range(1, parts):
            got = handed_on(msg, place)
            if place < parts - 1:
                c, msg = call(
                    functools.partial(hop_kernel, place), [vec, msg_shape],
                    got, c, msg, nr, d, js, ks, bnd,
                )
        c, tail, f = call(
            functools.partial(last_hop_kernel, parts - 1), [vec, longer, eight],
            got, c, nr, d, js, ks, ss,
        )
        for level, distance in enumerate(distances[:-1]):
            if step == 0:
                both = exchanged(jnp.concatenate([w, f], axis=0), distance)
                got = both[:width], both[width:]
                if level == 0:
                    w, f, kept["a", 0], bw, bf, aw, af = call(
                        functools.partial(first_level_kernel, distance),
                        [square, eight, square_split, square, eight, square, eight],
                        w, f, *got,
                    )
                else:
                    w, f, kept["a", level], kept["x", level], bw, bf, aw, af = call(
                        functools.partial(next_level_kernel, distance),
                        [square, eight, square_split, square_split, square, eight, square, eight],
                        w, f, *got, bw, bf, aw, af,
                    )
            else:
                got = exchanged(f, distance)
                if level == 0:
                    f, bf, af = call(
                        functools.partial(again_first_kernel, distance), [eight] * 3,
                        f, got, kept["a", 0],
                    )
                else:
                    f, bf, af = call(
                        functools.partial(again_next_kernel, distance), [eight] * 3,
                        f, got, bf, af, kept["a", level], kept["x", level],
                    )
        if step == 0:
            last = exchanged(jnp.concatenate([w, f], axis=0), distances[-1])
        else:
            last_f = exchanged(f, distances[-1])
        if step < ITERS - 1:
            base, v = call(local_kernel, [vec, longer], c, ls, tail, aw, af, s)
            s, nr, c, msg = call(
                turn_kernel, [vec, vec, vec, msg_shape],
                v, last, bw, bf, ps, base, halo, inj, cap, gain, gs, d, bnd,
            )
        else:
            (base,) = call(last_local_kernel, [vec], c, ls, tail, aw, af, last, bw, bf, ps, s)
            (s,) = call(end_kernel, [vec], last_f, bw, ps, base)
    return s[:, None]


def solution(mesh):
    in_specs = (
        P("tm", "dom", None),
        P("tm", "dom", None),
        P("dom", None),
        P("dom", None, None),
        P("dom", None, None),
        P("dom", None),
        P("dom", None, None),
        P("dom", None),
        P("tm", "dom", None, None, None),
        P("dom", None, None),
        P("tm", "dom", None, None, None),
    )
    out_specs = P("tm", "dom", None)
    return jax.shard_map(
        per_device, mesh=mesh, in_specs=in_specs, out_specs=out_specs, check_vma=False
    )
```

time: 56.6 us -> 50.1 us (0.89)
  waiting for transfers between devices: 16.3 us -> 30.8 us
  starting transfers between devices: 19.5 us -> 10.7 us
  local copies, waits for them, and re-layouts: 7.87 us -> 0.06 us
  Pallas kernels: 11.7 us -> 7.5 us
    ppermute x6, waiting for transfers between devices: 9.89 us -> 21.6 us  [exchanged(): lax.ppermute(v, 'tm', [(i, i ^ distance) for i in devices])]
    ppermute x6, starting transfers between devices: 11.6 us -> 3.03 us  [exchanged(): lax.ppermute(v, 'tm', [(i, i ^ distance) for i in devices])]
    unnamed x24 -> x20, local copies, waits for them, and re-layouts: 7.19 us -> 0.04 us
    pallas_call x19 -> x17, Pallas kernels: 11.7 us -> 7.5 us  [call(): pl.pallas_call(kernel, out_shape=[jax.ShapeDtypeStruct(s, d) for s, d in...]
    ppermute x1, waiting for transfers between devices: 0.01 us -> 2.01 us  [per_device(): lax.ppermute(starting_voltage_guess, 'tm', [(i, (i + 1) % segments) for i...]
    ppermute x6, waiting for transfers between devices: 6.43 us -> 7.22 us  [handed_on(): return lax.ppermute(message, 'dom', pairs)]
    slice x7 -> x4, local copies, waits for them, and re-layouts: 0.68 us -> 0.01 us  [per_device(): got = (both[:width], both[width:])]
  transfers between devices with their start and end apart: 13 -> 13, of which waited for: 10 -> 13; matrix products, arithmetic and copies ran while one was open for 0% -> 0% of each run, Pallas kernels for 10% -> 7%
where the time goes in v1:
time: 50.1 us; the launch traced here: 50 us
  waiting for transfers between devices  30.8 us (61%)
  starting transfers between devices  10.7 us (21%)
  Pallas kernels  7.5 us (15%)
  between operations  0.89 us (2%)
    ppermute x6, waiting for transfers between devices, exchanged(): lax.ppermute(v, 'tm', [(i, i ^ distance) for i in devices])  21.6 us
    pallas_call x17, Pallas kernels, call(): pl.pallas_call(kernel, out_shape=[jax.ShapeDtypeStruct(s, d) for s, d in...  7.5 us
    ppermute x6, waiting for transfers between devices, handed_on(): return lax.ppermute(message, 'dom', pairs)  7.22 us
    ppermute x6, starting transfers between devices, handed_on(): return lax.ppermute(message, 'dom', pairs)  4.65 us
    ppermute x1, starting transfers between devices, per_device(): lax.ppermute(starting_voltage_guess, 'tm', [(i, (i + 1) % segments) for i...  3.03 us
    ppermute x6, starting transfers between devices, exchanged(): lax.ppermute(v, 'tm', [(i, i ^ distance) for i in devices])  3.03 us
    ppermute x1, waiting for transfers between devices, per_device(): lax.ppermute(starting_voltage_guess, 'tm', [(i, (i + 1) % segments) for i...  2.01 us
  transfers between devices with their start and end apart: 13, of which 13 were waited for; matrix products, arithmetic and copies ran while one was open for 0% of the time, Pallas kernels for 7%

profile of v1, /device:TPU:0, one launch (start us, length us, event | category | flops | bytes accessed | tf_op | source)
XLA Modules:
  0.0 50.0 jit_solution(2414128434287578895)
XLA Ops:
  0.1 3.0 %collective-permute-start = (f32[16,1,128]{2,0,1:T(8,128)}, f32[16,1,128]{2,0,1:T(8,128)S(1)}, u32[]{:S(2)}, u32[]{:S(2)}) collective-permute-start(f32[16,1,128]{2,0,1:T(8,128)} %bitcast.24), channel_id=1, source_target_pairs={{0,4},{4,8},{8,12},{12,16},{16,20},{20,24},{24,28},{28,0},{1,5},{5... | collective-permute-start | bytes 24584 | tf_op jit(solution)/shard_map/ppermute | solution.py:365
  3.9 2.1 %shard_map.110 = (bf16[128,256]{1,0:T(8,128)(2,1)S(1)}, bf16[128,256]{1,0:T(8,128)(2,1)S(1)}, bf16[128,256]{1,0:T(8,128)(2,1)S(1)}, f32[16,128]{1,0:T(8,128)S(1)...) custom-call(f32[128,128]{1,0:T(8,128)S(1)} %shard_map.109.eye, ...), custom_call_target="tpu_custom_call" | custom-call | tf_op jit(solution)/shard_map/pallas_call | solution.py:59
  6.0 2.0 %collective-permute-done = f32[16,1,128]{2,0,1:T(8,128)S(1)} collective-permute-done((f32[16,1,128]{2,0,1:T(8,128)}, f32[16,1,128]{2,0,1:T(8,128)S(1)}, u32[]{:S(2)}, u32[]{:S(2)}) %collective-permute-start) | collective-permute-done | bytes 8224 | tf_op jit(solution)/shard_map/ppermute | solution.py:365
  8.0 0.2 shard_map.111
  8.2 1.2 %collective-permute-done.1.got_ref = f32[32,128]{1,0:T(8,128)S(1)} collective-permute-done((f32[32,128]{1,0:T(8,128)S(1)}, f32[32,128]{1,0:T(8,128)S(1)}, u32[]{:S(2)}, u32[]{:S(2)}) %collective-permute-start.1) | collective-permute-done | bytes 16416 | tf_op jit(solution)/shard_map/ppermute | solution.py:339
  9.4 1.4 %collective-permute-start.2 = (f32[32,128]{1,0:T(8,128)S(1)}, f32[32,128]{1,0:T(8,128)S(1)}, u32[]{:S(2)}, u32[]{:S(2)}) collective-permute-start(f32[32,128]{1,0:T(8,128)S(1)} %get-tuple-element.66.msg_ref), channel_id=1, source_target_pairs={{1,2},{2,1},{3,0},{0,3},{5,6},{6,5},{7,4},{4,7},{9,10},{10,9},{11,... | collective-permute-start | bytes 49160 | tf_op jit(solution)/shard_map/ppermute | solution.py:339
  10.8 1.7 %collective-permute-done.2.got_ref = f32[32,128]{1,0:T(8,128)S(1)} collective-permute-done((f32[32,128]{1,0:T(8,128)S(1)}, f32[32,128]{1,0:T(8,128)S(1)}, u32[]{:S(2)}, u32[]{:S(2)}) %collective-permute-start.2) | collective-permute-done | bytes 16416 | tf_op jit(solution)/shard_map/ppermute | solution.py:339
  12.5 0.7 %collective-permute-start.3 = (f32[32,128]{1,0:T(8,128)S(1)}, f32[32,128]{1,0:T(8,128)S(1)}, u32[]{:S(2)}, u32[]{:S(2)}) collective-permute-start(f32[32,128]{1,0:T(8,128)S(1)} %get-tuple-element.68), channel_id=1, source_target_pairs={{2,3},{3,2},{0,1},{1,0},{6,7},{7,6},{4,5},{5,4},{10,11},{11,10},{8... | collective-permute-start | bytes 49160 | tf_op jit(solution)/shard_map/ppermute | solution.py:339
  13.3 0.8 %collective-permute-done.3.got_ref = f32[32,128]{1,0:T(8,128)S(1)} collective-permute-done((f32[32,128]{1,0:T(8,128)S(1)}, f32[32,128]{1,0:T(8,128)S(1)}, u32[]{:S(2)}, u32[]{:S(2)}) %collective-permute-start.3) | collective-permute-done | bytes 16416 | tf_op jit(solution)/shard_map/ppermute | solution.py:339
  14.1 0.4 shard_map.114
  14.6 4.4 %collective-permute-done.4 = f32[136,128]{1,0:T(8,128)S(1)} collective-permute-done((f32[136,128]{1,0:T(8,128)S(1)}, f32[136,128]{1,0:T(8,128)S(1)}, u32[]{:S(2)}, u32[]{:S(2)}) %collective-permute-start.4) | collective-permute-done | bytes 69664 | tf_op jit(solution)/shard_map/ppermute | solution.py:330
  19.0 0.2 shard_map.115
  19.3 4.3 %collective-permute-done.5 = f32[136,128]{1,0:T(8,128)S(1)} collective-permute-done((f32[136,128]{1,0:T(8,128)S(1)}, f32[136,128]{1,0:T(8,128)S(1)}, u32[]{:S(2)}, u32[]{:S(2)}) %collective-permute-start.5) | collective-permute-done | bytes 69664 | tf_op jit(solution)/shard_map/ppermute | solution.py:330
  23.6 0.2 shard_map.116
  23.9 1.0 %collective-permute-start.6 = (f32[136,128]{1,0:T(8,128)S(1)}, f32[136,128]{1,0:T(8,128)S(1)}, u32[]{:S(2)}, u32[]{:S(2)}) collective-permute-start(f32[136,128]{1,0:T(8,128)S(1)} %pad_maximum_fusion.2), channel_id=1, source_target_pairs={{0,16},{4,20},{8,24},{12,28},{16,0},{20,4},{24,8},{28,12},{1,17},{... | collective-permute-start | bytes 208904 | tf_op jit(solution)/shard_map/ppermute | solution.py:330
  24.9 0.6 %shard_map.117 = (f32[16,128]{1,0:T(8,128)S(1)}, f32[24,128]{1,0:T(8,128)S(1)}) custom-call(f32[16,128]{1,0:T(8,128)S(1)} %get-tuple-element.71.c_ref, f32[32,128,128]{2,1,0:T(8,128)S(1)} %get-tuple-element.72.ls_ref, f32[24,128]{1,0:T(8,128)S(1)} %get-tuple-element.73.tail_ref, f32[128,128]{1,0:T(8,128)S(1)} %get-tuple-element.82.aw_ref, ...), custom_call_target="tpu_custom_call" | custom-call | tf_op jit(solution)/shard_map/pallas_call | solution.py:59
  25.5 3.8 %collective-permute-done.6.got_ref.gw_ref = f32[136,128]{1,0:T(8,128)S(1)} collective-permute-done((f32[136,128]{1,0:T(8,128)S(1)}, f32[136,128]{1,0:T(8,128)S(1)}, u32[]{:S(2)}, u32[]{:S(2)}) %collective-permute-start.6) | collective-permute-done | bytes 69664 | tf_op jit(solution)/shard_map/ppermute | solution.py:330
  29.3 1.2 %shard_map.118 = (f32[16,128]{1,0:T(8,128)S(1)}, f32[16,128]{1,0:T(8,128)S(1)}, f32[16,128]{1,0:T(8,128)S(1)}, f32[32,128]{1,0:T(8,128)S(1)}) custom-call(f32[24,128]{1,0:T(8,128)S(1)} %get-tuple-element.84.v_ref, f32[136,128]{1,0:T(8,128)S(1)} %collective-permute-done.6.got_ref.gw_ref, f32[128,128]{1,0:T(8,128)S(1)} %get-tuple-element.87.bw_ref, ...), custom_call_target="tpu_custom_call" | custom-call | tf_op jit(solution)/shard_map/pallas_call | solution.py:59
  30.5 1.2 %collective-permute-done.7.got_ref = f32[32,128]{1,0:T(8,128)S(1)} collective-permute-done((f32[32,128]{1,0:T(8,128)S(1)}, f32[32,128]{1,0:T(8,128)S(1)}, u32[]{:S(2)}, u32[]{:S(2)}) %collective-permute-start.7) | collective-permute-done | bytes 16416 | tf_op jit(solution)/shard_map/ppermute | solution.py:339
  31.7 1.9 %collective-permute-start.8 = (f32[32,128]{1,0:T(8,128)S(1)}, f32[32,128]{1,0:T(8,128)S(1)}, u32[]{:S(2)}, u32[]{:S(2)}) collective-permute-start(f32[32,128]{1,0:T(8,128)S(1)} %get-tuple-element.96.msg_ref), channel_id=1, source_target_pairs={{1,2},{2,1},{3,0},{0,3},{5,6},{6,5},{7,4},{4,7},{9,10},{10,9},{11,... | collective-permute-start | bytes 49160 | tf_op jit(solution)/shard_map/ppermute | solution.py:339
  33.6 1.4 %collective-permute-done.8.got_ref = f32[32,128]{1,0:T(8,128)S(1)} collective-permute-done((f32[32,128]{1,0:T(8,128)S(1)}, f32[32,128]{1,0:T(8,128)S(1)}, u32[]{:S(2)}, u32[]{:S(2)}) %collective-permute-start.8) | collective-permute-done | bytes 16416 | tf_op jit(solution)/shard_map/ppermute | solution.py:339
  35.0 0.5 %collective-permute-start.9 = (f32[32,128]{1,0:T(8,128)S(1)}, f32[32,128]{1,0:T(8,128)S(1)}, u32[]{:S(2)}, u32[]{:S(2)}) collective-permute-start(f32[32,128]{1,0:T(8,128)S(1)} %get-tuple-element.98), channel_id=1, source_target_pairs={{2,3},{3,2},{0,1},{1,0},{6,7},{7,6},{4,5},{5,4},{10,11},{11,10},{8... | collective-permute-start | bytes 49160 | tf_op jit(solution)/shard_map/ppermute | solution.py:339
  35.6 0.8 %collective-permute-done.9.got_ref = f32[32,128]{1,0:T(8,128)S(1)} collective-permute-done((f32[32,128]{1,0:T(8,128)S(1)}, f32[32,128]{1,0:T(8,128)S(1)}, u32[]{:S(2)}, u32[]{:S(2)}) %collective-permute-start.9) | collective-permute-done | bytes 16416 | tf_op jit(solution)/shard_map/ppermute | solution.py:339
  36.4 0.4 shard_map.121
  36.8 0.9 %collective-permute-start.10 = (f32[8,128]{1,0:T(8,128)S(1)}, f32[8,128]{1,0:T(8,128)S(1)}, u32[]{:S(2)}, u32[]{:S(2)}) collective-permute-start(f32[8,128]{1,0:T(8,128)S(1)} %get-tuple-element.100.mf_ref), channel_id=1, source_target_pairs={{0,4},{4,0},{8,12},{12,8},{16,20},{20,16},{24,28},{28,24},{1,5},{5... | collective-permute-start | bytes 12296 | tf_op jit(solution)/shard_map/ppermute | solution.py:330
  37.7 2.8 %collective-permute-done.10.gf_ref = f32[8,128]{1,0:T(8,128)S(1)} collective-permute-done((f32[8,128]{1,0:T(8,128)S(1)}, f32[8,128]{1,0:T(8,128)S(1)}, u32[]{:S(2)}, u32[]{:S(2)}) %collective-permute-start.10) | collective-permute-done | bytes 4128 | tf_op jit(solution)/shard_map/ppermute | solution.py:330
  40.6 3.6 %collective-permute-done.11.gf_ref = f32[8,128]{1,0:T(8,128)S(1)} collective-permute-done((f32[8,128]{1,0:T(8,128)S(1)}, f32[8,128]{1,0:T(8,128)S(1)}, u32[]{:S(2)}, u32[]{:S(2)}) %collective-permute-start.11) | collective-permute-done | bytes 4128 | tf_op jit(solution)/shard_map/ppermute | solution.py:330
  44.2 0.1 shard_map.123
  44.4 1.0 %collective-permute-start.12 = (f32[8,128]{1,0:T(8,128)S(1)}, f32[8,128]{1,0:T(8,128)S(1)}, u32[]{:S(2)}, u32[]{:S(2)}) collective-permute-start(f32[8,128]{1,0:T(8,128)S(1)} %get-tuple-element.107), channel_id=1, source_target_pairs={{0,16},{4,20},{8,24},{12,28},{16,0},{20,4},{24,8},{28,12},{1,17},{... | collective-permute-start | bytes 12296 | tf_op jit(solution)/shard_map/ppermute | solution.py:330
  45.3 0.9 %shard_map.124.base_ref = f32[16,128]{1,0:T(8,128)S(1)} custom-call(f32[16,128]{1,0:T(8,128)S(1)} %get-tuple-element.108.c_ref, f32[32,128,128]{2,1,0:T(8,128)S(1)} %get-tuple-element.72.ls_ref, f32[24,128]{1,0:T(8,128)S(1)} %get-tuple-element.109.tail_ref, f32[128,128]{1,0:T(8,128)S(1)} %get-tuple-element.82.aw_ref, ...), custom_call_target="tpu_custom_call" | custom-call | tf_op jit(solution)/shard_map/pallas_call | solution.py:59
  46.2 2.7 %collective-permute-done.12.gf_ref = f32[8,128]{1,0:T(8,128)S(1)} collective-permute-done((f32[8,128]{1,0:T(8,128)S(1)}, f32[8,128]{1,0:T(8,128)S(1)}, u32[]{:S(2)}, u32[]{:S(2)}) %collective-permute-start.12) | collective-permute-done | bytes 4128 | tf_op jit(solution)/shard_map/ppermute | solution.py:330
  48.9 1.1 %shard_map.125 = f32[16,128]{1,0:T(8,128)} custom-call(f32[8,128]{1,0:T(8,128)S(1)} %collective-permute-done.12.gf_ref, f32[128,128]{1,0:T(8,128)S(1)} %get-tuple-element.87.bw_ref, f32[16,128,128]{2,1,0:T(8,128)S(1)} %get-tuple-element.89.ps_ref, f32[16,128]{1,0:T(8,128)S(1)} %shard_map.124.base_ref), custom_call_target="tpu_custom_call" | custom-call | tf_op jit(solution)/shard_map/pallas_call | solution.py:59
  (38 shorter events, 0.4 us)
Async XLA Ops:
  0.0 3.8 %copy-start = (f32[16,1,1,128,128]{4,3,2,1,0:T(8,128)S(1)}, f32[16,1,1,128,128]{4,3,2,1,0:T(8,128)}, u32[]{:S(2)}) copy-start(f32[16,1,1,128,128]{4,3,2,1,0:T(8,128)} %param.19) | copy-start | bytes 3145732
  0.0 3.8 %copy-start.1 = (f32[16,1,1,128,128]{4,3,2,1,0:T(8,128)S(1)}, f32[16,1,1,128,128]{4,3,2,1,0:T(8,128)}, u32[]{:S(2)}) copy-start(f32[16,1,1,128,128]{4,3,2,1,0:T(8,128)} %param.21) | copy-start | bytes 3145732
  0.0 3.8 %copy-start.2 = (f32[16,1,128]{2,1,0:T(1,128)S(1)}, f32[16,1,128]{2,1,0:T(1,128)}, u32[]{:S(2)}) copy-start(f32[16,1,128]{2,1,0:T(1,128)} %param.11) | copy-start | bytes 24580
  0.0 3.8 %copy-start.3 = (f32[1,128,128]{2,1,0:T(8,128)S(1)}, f32[1,128,128]{2,1,0:T(8,128)}, u32[]{:S(2)}) copy-start(f32[1,128,128]{2,1,0:T(8,128)} %param.14) | copy-start | bytes 196612
  0.0 3.8 %copy-start.4 = (f32[1,128,128]{2,1,0:T(8,128)S(1)}, f32[1,128,128]{2,1,0:T(8,128)}, u32[]{:S(2)}) copy-start(f32[1,128,128]{2,1,0:T(8,128)} %param.17) | copy-start | bytes 196612
  0.0 3.8 %copy-start.5 = (f32[1,128,128]{2,1,0:T(8,128)S(1)}, f32[1,128,128]{2,1,0:T(8,128)}, u32[]{:S(2)}) copy-start(f32[1,128,128]{2,1,0:T(8,128)} %param.20) | copy-start | bytes 196612
  0.0 3.8 %copy-start.6 = (f32[16,1,128]{2,1,0:T(1,128)S(1)}, f32[16,1,128]{2,1,0:T(1,128)}, u32[]{:S(2)}) copy-start(f32[16,1,128]{2,1,0:T(1,128)} %param.12) | copy-start | bytes 24580
  0.0 3.8 %copy-start.8 = (f32[1,128]{1,0:T(1,128)S(1)}, f32[1,128]{1,0:T(1,128)}, u32[]{:S(2)}) copy-start(f32[1,128]{1,0:T(1,128)} %cap_ref.3) | copy-start | bytes 1540
  0.0 3.8 %copy-start.9 = (f32[1,128]{1,0:T(1,128)S(1)}, f32[1,128]{1,0:T(1,128)}, u32[]{:S(2)}) copy-start(f32[1,128]{1,0:T(1,128)} %gain_ref.1) | copy-start | bytes 1540
  0.1 7.9 %collective-permute-start = (f32[16,1,128]{2,0,1:T(8,128)}, f32[16,1,128]{2,0,1:T(8,128)S(1)}, u32[]{:S(2)}, u32[]{:S(2)}) collective-permute-start(f32[16,1,128]{2,0,1:T(8,128)} %bitcast.24), channel_id=1, source_target_pairs={{0,4},{4,8},{8,12},{12,16},{16,20},{20,24},{24,28},{28,0},{1,5},{5... | collective-permute-start | bytes 24584 | tf_op jit(solution)/shard_map/ppermute | solution.py:365
  3.1 4.9 %copy-start.7 = (s32[1,128]{1,0:T(1,128)S(1)}, s32[1,128]{1,0:T(1,128)}, u32[]{:S(2)}) copy-start(s32[1,128]{1,0:T(1,128)} %bnd_ref.11) | copy-start | bytes 1540
  8.1 1.2 %collective-permute-start.1 = (f32[32,128]{1,0:T(8,128)S(1)}, f32[32,128]{1,0:T(8,128)S(1)}, u32[]{:S(2)}, u32[]{:S(2)}) collective-permute-start(f32[32,128]{1,0:T(8,128)S(1)} %get-tuple-element.61.msg_ref), channel_id=1, source_target_pairs={{0,1},{1,0},{2,3},{3,2},{4,5},{5,4},{6,7},{7,6},{8,9},{9,8},{10,11... | collective-permute-start | bytes 49160 | tf_op jit(solution)/shard_map/ppermute | solution.py:339
  9.4 3.2 %collective-permute-start.2 = (f32[32,128]{1,0:T(8,128)S(1)}, f32[32,128]{1,0:T(8,128)S(1)}, u32[]{:S(2)}, u32[]{:S(2)}) collective-permute-start(f32[32,128]{1,0:T(8,128)S(1)} %get-tuple-element.66.msg_ref), channel_id=1, source_target_pairs={{1,2},{2,1},{3,0},{0,3},{5,6},{6,5},{7,4},{4,7},{9,10},{10,9},{11,... | collective-permute-start | bytes 49160 | tf_op jit(solution)/shard_map/ppermute | solution.py:339
  12.5 1.6 %collective-permute-start.3 = (f32[32,128]{1,0:T(8,128)S(1)}, f32[32,128]{1,0:T(8,128)S(1)}, u32[]{:S(2)}, u32[]{:S(2)}) collective-permute-start(f32[32,128]{1,0:T(8,128)S(1)} %get-tuple-element.68), channel_id=1, source_target_pairs={{2,3},{3,2},{0,1},{1,0},{6,7},{7,6},{4,5},{5,4},{10,11},{11,10},{8... | collective-permute-start | bytes 49160 | tf_op jit(solution)/shard_map/ppermute | solution.py:339
  14.5 4.5 %collective-permute-start.4 = (f32[136,128]{1,0:T(8,128)S(1)}, f32[136,128]{1,0:T(8,128)S(1)}, u32[]{:S(2)}, u32[]{:S(2)}) collective-permute-start(f32[136,128]{1,0:T(8,128)S(1)} %pad_maximum_fusion), channel_id=1, source_target_pairs={{0,4},{4,0},{8,12},{12,8},{16,20},{20,16},{24,28},{28,24},{1,5},{5... | collective-permute-start | bytes 208904 | tf_op jit(solution)/shard_map/ppermute | solution.py:330
  19.2 4.4 %collective-permute-start.5 = (f32[136,128]{1,0:T(8,128)S(1)}, f32[136,128]{1,0:T(8,128)S(1)}, u32[]{:S(2)}, u32[]{:S(2)}) collective-permute-start(f32[136,128]{1,0:T(8,128)S(1)} %pad_maximum_fusion.1), channel_id=1, source_target_pairs={{0,8},{4,12},{8,0},{12,4},{16,24},{20,28},{24,16},{28,20},{1,9},{5... | collective-permute-start | bytes 208904 | tf_op jit(solution)/shard_map/ppermute | solution.py:330
  23.9 5.5 %collective-permute-start.6 = (f32[136,128]{1,0:T(8,128)S(1)}, f32[136,128]{1,0:T(8,128)S(1)}, u32[]{:S(2)}, u32[]{:S(2)}) collective-permute-start(f32[136,128]{1,0:T(8,128)S(1)} %pad_maximum_fusion.2), channel_id=1, source_target_pairs={{0,16},{4,20},{8,24},{12,28},{16,0},{20,4},{24,8},{28,12},{1,17},{... | collective-permute-start | bytes 208904 | tf_op jit(solution)/shard_map/ppermute | solution.py:330
  30.5 1.2 %collective-permute-start.7 = (f32[32,128]{1,0:T(8,128)S(1)}, f32[32,128]{1,0:T(8,128)S(1)}, u32[]{:S(2)}, u32[]{:S(2)}) collective-permute-start(f32[32,128]{1,0:T(8,128)S(1)} %get-tuple-element.93.msg_ref), channel_id=1, source_target_pairs={{0,1},{1,0},{2,3},{3,2},{4,5},{5,4},{6,7},{7,6},{8,9},{9,8},{10,11... | collective-permute-start | bytes 49160 | tf_op jit(solution)/shard_map/ppermute | solution.py:339
  31.7 3.4 %collective-permute-start.8 = (f32[32,128]{1,0:T(8,128)S(1)}, f32[32,128]{1,0:T(8,128)S(1)}, u32[]{:S(2)}, u32[]{:S(2)}) collective-permute-start(f32[32,128]{1,0:T(8,128)S(1)} %get-tuple-element.96.msg_ref), channel_id=1, source_target_pairs={{1,2},{2,1},{3,0},{0,3},{5,6},{6,5},{7,4},{4,7},{9,10},{10,9},{11,... | collective-permute-start | bytes 49160 | tf_op jit(solution)/shard_map/ppermute | solution.py:339
  35.0 1.4 %collective-permute-start.9 = (f32[32,128]{1,0:T(8,128)S(1)}, f32[32,128]{1,0:T(8,128)S(1)}, u32[]{:S(2)}, u32[]{:S(2)}) collective-permute-start(f32[32,128]{1,0:T(8,128)S(1)} %get-tuple-element.98), channel_id=1, source_target_pairs={{2,3},{3,2},{0,1},{1,0},{6,7},{7,6},{4,5},{5,4},{10,11},{11,10},{8... | collective-permute-start | bytes 49160 | tf_op jit(solution)/shard_map/ppermute | solution.py:339
  36.8 3.7 %collective-permute-start.10 = (f32[8,128]{1,0:T(8,128)S(1)}, f32[8,128]{1,0:T(8,128)S(1)}, u32[]{:S(2)}, u32[]{:S(2)}) collective-permute-start(f32[8,128]{1,0:T(8,128)S(1)} %get-tuple-element.100.mf_ref), channel_id=1, source_target_pairs={{0,4},{4,0},{8,12},{12,8},{16,20},{20,16},{24,28},{28,24},{1,5},{5... | collective-permute-start | bytes 12296 | tf_op jit(solution)/shard_map/ppermute | solution.py:330
  40.6 3.6 %collective-permute-start.11 = (f32[8,128]{1,0:T(8,128)S(1)}, f32[8,128]{1,0:T(8,128)S(1)}, u32[]{:S(2)}, u32[]{:S(2)}) collective-permute-start(f32[8,128]{1,0:T(8,128)S(1)} %get-tuple-element.102.mf_ref), channel_id=1, source_target_pairs={{0,8},{4,12},{8,0},{12,4},{16,24},{20,28},{24,16},{28,20},{1,9},{5... | collective-permute-start | bytes 12296 | tf_op jit(solution)/shard_map/ppermute | solution.py:330
  44.4 4.5 %collective-permute-start.12 = (f32[8,128]{1,0:T(8,128)S(1)}, f32[8,128]{1,0:T(8,128)S(1)}, u32[]{:S(2)}, u32[]{:S(2)}) collective-permute-start(f32[8,128]{1,0:T(8,128)S(1)} %get-tuple-element.107), channel_id=1, source_target_pairs={{0,16},{4,20},{8,24},{12,28},{16,0},{20,4},{24,8},{28,12},{1,17},{... | collective-permute-start | bytes 12296 | tf_op jit(solution)/shard_map/ppermute | solution.py:330
